TPU v7x, 32 devices: a whole 2x2x4 slice. The times are simulated.
32 devices in a mesh: slab: 2 (over x), plane: 8 (over z, y), brick: 2 (over core).
Axes of the slice: x: 2, y: 2, z: 4, core: 2. Of those that a mesh axis runs over, the one named last changes fastest.
Arguments:
- camera_rows: bfloat16 [4, 16, 32, 2048], P(None, 'slab', ('plane', 'brick')), parts along dimension 1, may hold values from 0.19921875 to 5
- estimate: float32 [16, 32, 2048], P('slab', None, ('plane', 'brick')), parts along dimension 0, may hold values from 0.2 to 5
- psf_bank: float32 [32, 4, 3, 31], P(('slab', 'plane', 'brick')), parts along dimension 0, may hold values from 0 to 1.25, as said below
- psf_owner: int32 [32], P('slab'), parts along dimension 0, may hold values from 0 to 15, each once
- view_mask: int32 [32, 4], P('slab'), parts along dimension 0, may hold values 0 or 1
Outputs:
- deconvolved: float32 [16, 32, 2048], P('slab', None, ('plane', 'brick')), parts along dimension 0
There are 2 independent parts, one for each index of `slab`. A program takes and returns all parts, laid end to end along the dimension named above; each array names one. Nothing has to cross between parts.
Inputs may be any that keep to these rules, and one draw needn't show every extreme that they name: `psf_owner`: every brick names a different device: the map is a permutation of 0 to 15. `psf_bank`: every tap is positive.
All inputs are finite; a program needn't handle non-finite values.
Results may differ from a plain program's by a relative error of at most 0.0003.
Values may be sent and summed in bfloat16 or wider, within the bound.
A program may use at most 192 MiB of HBM per device.

v0:
```python
import jax
import jax.numpy as jnp
from jax import lax
from jax.sharding import PartitionSpec as P

V = 4
RADIUS = 15
ITERS = 2
BACKGROUND = 0.1
HIGHEST = lax.Precision.HIGHEST


def padded_2(cells, sides, width):
    for axis, dim in sides:
        count = lax.axis_size(axis)
        ends = count - 1
        head = lax.slice_in_dim(cells, 0, width, axis=dim)
        tail = lax.slice_in_dim(cells, cells.shape[dim] - width, cells.shape[dim], axis=dim)
        cells = jnp.concatenate(
            [
                lax.ppermute(tail, axis, [(i, (i + 1) % count) for i in range(ends)]),
                cells,
                lax.ppermute(head, axis, [((i + 1) % count, i) for i in range(ends)]),
            ],
            axis=dim,
        )
    return cells


def banded(profiles, size_in, size_out, offset):
    tap_count = profiles.shape[-1]
    centre = tap_count // 2
    lag_index = (
        jnp.arange(size_in, dtype=jnp.int32)[:, None]
        - jnp.arange(size_out, dtype=jnp.int32)[None, :]
        - offset
        + centre
    )
    one_hot = (
        lag_index[:, :, None] == jnp.arange(tap_count, dtype=jnp.int32)[None, None, :]
    ).astype(jnp.float32)
    return jnp.einsum("ijt,vt->vij", one_hot, profiles, precision=HIGHEST)


def across_columns(volume, band_x):
    if volume.ndim == 3:
        return jnp.einsum("zyi,vij->vzyj", volume, band_x, precision=HIGHEST)
    return jnp.einsum("vzyi,vij->vzyj", volume, band_x, precision=HIGHEST)


def across_rows(volume, band_y):
    view_count, depth_count, row_count, col_count = volume.shape
    block_rows = band_y.shape[2]
    margin = (band_y.shape[1] - block_rows) // 2
    pieces = volume.reshape(view_count, depth_count, row_count // block_rows, block_rows, col_count)
    blanks = jnp.zeros((view_count, depth_count, 1, margin, col_count), jnp.float32)
    before = jnp.concatenate([blanks, pieces[:, :, :-1, block_rows - margin :, :]], axis=2)
    behind = jnp.concatenate([pieces[:, :, 1:, :margin, :], blanks], axis=2)
    windows = jnp.concatenate([before, pieces, behind], axis=3)
    result = jnp.einsum("vzqic,vij->vzqjc", windows, band_y, precision=HIGHEST)
    return result.reshape(view_count, depth_count, row_count, col_count)


def across_depth(volume, band_z):
    return jnp.einsum("vzyc,vzw->vwyc", volume, band_z, precision=HIGHEST)


def separable(volume, bands):
    return across_depth(across_rows(across_columns(volume, bands[0]), bands[1]), bands[2])


def shards(camera_rows, estimate, psf_bank, psf_owner, view_mask):
    regrouped = lax.all_to_all(
        camera_rows, ("plane", "brick"), split_axis=3, concat_axis=2, tiled=True
    )
    position = lax.axis_index(("plane", "brick"))
    brick_ids = jnp.arange(psf_owner.shape[0], dtype=jnp.int32)
    is_mine = brick_ids == position
    owner_id = jnp.sum(jnp.where(is_mine, psf_owner, 0))
    observed = jnp.sum(jnp.where(is_mine[:, None], view_mask, 0), axis=0) > 0
    fitted = lax.all_gather(psf_bank, ("plane", "brick"), axis=0, tiled=True)
    chosen = (brick_ids == owner_id).astype(jnp.float32)
    kernels = jnp.einsum("b,bvat->vat", chosen, fitted, precision=HIGHEST)
    kernels = kernels / jnp.sum(kernels, axis=-1, keepdims=True)
    flipped = kernels[:, :, ::-1]
    depth_size = estimate.shape[0]
    row_size = estimate.shape[1]
    col_size = estimate.shape[2]
    block_size = 128 if row_size % 128 == 0 else row_size

    def make_bands(profiles):
        return (
            banded(profiles[:, 2], col_size + 2 * RADIUS, col_size, RADIUS),
            banded(profiles[:, 1], block_size + 2 * RADIUS, block_size, RADIUS),
            banded(profiles[:, 0], depth_size, depth_size, 0),
        )

    blur_bands = make_bands(kernels)
    back_bands = make_bands(flipped)
    current = estimate
    for iteration in range(ITERS):
        padded = padded_2(current.astype(jnp.bfloat16), ((("plane", "brick"), 2),), RADIUS).astype(
            current.dtype
        )
        blurred = separable(padded, blur_bands)
        quotient = jnp.where(
            observed[:, None, None, None],
            regrouped.astype(jnp.float32) / (blurred + BACKGROUND),
            0.0,
        )
        quotient_wide = padded_2(
            quotient.astype(jnp.bfloat16), ((("plane", "brick"), 3),), RADIUS
        ).astype(quotient.dtype)
        corrected = separable(quotient_wide, back_bands)
        factor = jnp.sum(jnp.where(observed[:, None, None, None], corrected, 1.0), axis=0) / V
        current = current * factor
    return current


def solution(mesh):
    return jax.shard_map(
        shards,
        mesh=mesh,
        in_specs=(
            P(None, "slab", ("plane", "brick"), None),
            P("slab", None, ("plane", "brick")),
            P(("slab", "plane", "brick"), None, None, None),
            P("slab"),
            P("slab", None),
        ),
        out_specs=P("slab", None, ("plane", "brick")),
        check_vma=False,
    )
```

profile of v0, /device:TPU:1, one launch (start us, length us, event | category | flops | bytes accessed | tf_op | source)
XLA Modules:
  0.0 100.3 jit_solution(6253015987272240798)
XLA Ops:
  0.0 6.3 %copy.47 = bf16[4,8,2,2048]{1,0,2,3:T(4,128)(2,1)} copy(bf16[4,8,2,2048]{3,2,1,0:T(2,128)(2,1)} %param.5) | data formatting | bytes 524288 | tf_op args[0]
  6.4 6.5 %reshape.127 = bf16[16,2,4096]{2,1,0:T(2,128)(2,1)} reshape(bf16[2048,2,4,8]{3,2,1,0:T(4,128)(2,1)} %bitcast.116) | data formatting | bytes 524288
  12.8 7.3 %all-to-all-start = ((bf16[16,2,4096]{2,1,0:T(2,128)(2,1)}), bf16[16,2,4096]{2,1,0:T(2,128)(2,1)S(1)}, u32[]{:S(2)}, u32[]{:S(2)}) async-start(bf16[16,2,4096]{2,1,0:T(2,128)(2,1)} %reshape.127), calls=%async_computation | async-start | bytes 524288 | tf_op jit(solution)/shard_map/all_to_all | solution.py:73
  20.3 2.0 %collective-permute-start.1 = (bf16[8,32,15]{2,1,0:T(8,128)(2,1)S(1)}, bf16[8,32,15]{2,1,0:T(8,128)(2,1)S(1)}, u32[]{:S(2)}, u32[]{:S(2)}) collective-permute-start(bf16[8,32,15]{2,1,0:T(8,128)(2,1)S(1)} %get-tuple-element.12), channel_id=1, source_target_pairs={{1,0},{2,1},{3,2},{4,3},{5,4},{6,5},{7,6},{8,7},{9,8},{10,9},{11,1... | collective-permute-start | bytes 23048 | tf_op jit(solution)/shard_map/ppermute | solution.py:23
  22.3 3.5 %collective-permute-start = (bf16[8,32,15]{2,1,0:T(8,128)(2,1)S(1)}, bf16[8,32,15]{2,1,0:T(8,128)(2,1)S(1)}, u32[]{:S(2)}, u32[]{:S(2)}) collective-permute-start(bf16[8,32,15]{2,1,0:T(8,128)(2,1)S(1)} %get-tuple-element.11), channel_id=1, source_target_pairs={{0,1},{1,2},{2,3},{3,4},{4,5},{5,6},{6,7},{7,8},{8,9},{9,10},{10,1... | collective-permute-start | bytes 23048 | tf_op jit(solution)/shard_map/ppermute | solution.py:21
  25.9 20.7 %all_gather.3 = f32[16,4,3,31]{3,1,2,0:T(4,128)S(1)} all-gather(f32[1,4,3,31]{3,1,2,0:T(4,128)S(1)} %copy-done.1), channel_id=1, replica_groups=mesh['slab'=2,'plane'=8,'brick'=2] {'plane','brick'}, dimensions={0}, use_global_device_ids=true | all-gather | bytes 25296 | tf_op jit(solution)/shard_map/all_gather | solution.py:81
  48.2 0.9 fusion.12
  49.6 0.9 fusion.13
  52.7 5.9 %reshape.128 = bf16[2048,2,4,8]{3,2,1,0:T(4,128)(2,1)} reshape(bf16[16,2,4096]{2,1,0:T(2,128)(2,1)S(1)} %all-to-all-done) | data formatting | bytes 524288
  58.7 5.9 %copy.48 = f32[4,8,2,16,128]{4,1,2,3,0:T(8,128)S(1)} copy(bf16[4,8,2,16,128]{1,0,2,4,3:T(4,128)(2,1)} %bitcast.115) | data formatting | bytes 786432 | tf_op jit(solution)/shard_map/convert_element_type | solution.py:108
  64.6 0.9 fusion.8
  65.6 2.1 %collective-permute-start.3 = (bf16[4,8,32,15]{3,1,2,0:T(8,128)(2,1)S(1)}, bf16[4,8,32,15]{3,1,2,0:T(8,128)(2,1)S(1)}, u32[]{:S(2)}, u32[]{:S(2)}) collective-permute-start(bf16[4,8,32,15]{3,1,2,0:T(8,128)(2,1)S(1)} %get-tuple-element.8), channel_id=1, source_target_pairs={{1,0},{2,1},{3,2},{4,3},{5,4},{6,5},{7,6},{8,7},{9,8},{10,9},{11,1... | collective-permute-start | bytes 92168 | tf_op jit(solution)/shard_map/ppermute | solution.py:23
  67.7 3.5 %collective-permute-start.2 = (bf16[4,8,32,15]{3,1,2,0:T(8,128)(2,1)S(1)}, bf16[4,8,32,15]{3,1,2,0:T(8,128)(2,1)S(1)}, u32[]{:S(2)}, u32[]{:S(2)}) collective-permute-start(bf16[4,8,32,15]{3,1,2,0:T(8,128)(2,1)S(1)} %get-tuple-element.7), channel_id=1, source_target_pairs={{0,1},{1,2},{2,3},{3,4},{4,5},{5,6},{6,7},{7,8},{8,9},{9,10},{10,1... | collective-permute-start | bytes 92168 | tf_op jit(solution)/shard_map/ppermute | solution.py:21
  71.7 1.6 %collective-permute-done.3 = bf16[4,8,32,15]{3,1,2,0:T(8,128)(2,1)S(1)} collective-permute-done((bf16[4,8,32,15]{3,1,2,0:T(8,128)(2,1)S(1)}, bf16[4,8,32,15]{3,1,2,0:T(8,128)(2,1)S(1)}, u32[]{:S(2)}, u32[]{:S(2)}) %collective-permute-start.3) | collective-permute-done | bytes 30752 | tf_op jit(solution)/shard_map/ppermute | solution.py:23
  73.3 1.2 %collective-permute-done.2 = bf16[4,8,32,15]{3,1,2,0:T(8,128)(2,1)S(1)} collective-permute-done((bf16[4,8,32,15]{3,1,2,0:T(8,128)(2,1)S(1)}, bf16[4,8,32,15]{3,1,2,0:T(8,128)(2,1)S(1)}, u32[]{:S(2)}, u32[]{:S(2)}) %collective-permute-start.2) | collective-permute-done | bytes 30752 | tf_op jit(solution)/shard_map/ppermute | solution.py:21
  76.1 0.8 fusion.10
  77.1 1.9 %collective-permute-start.5 = (bf16[8,32,15]{2,1,0:T(8,128)(2,1)S(1)}, bf16[8,32,15]{2,1,0:T(8,128)(2,1)S(1)}, u32[]{:S(2)}, u32[]{:S(2)}) collective-permute-start(bf16[8,32,15]{2,1,0:T(8,128)(2,1)S(1)} %get-tuple-element.10), channel_id=1, source_target_pairs={{1,0},{2,1},{3,2},{4,3},{5,4},{6,5},{7,6},{8,7},{9,8},{10,9},{11,1... | collective-permute-start | bytes 23048 | tf_op jit(solution)/shard_map/ppermute | solution.py:23
  79.0 4.6 %collective-permute-start.4 = (bf16[8,32,15]{2,1,0:T(8,128)(2,1)S(1)}, bf16[8,32,15]{2,1,0:T(8,128)(2,1)S(1)}, u32[]{:S(2)}, u32[]{:S(2)}) collective-permute-start(bf16[8,32,15]{2,1,0:T(8,128)(2,1)S(1)} %get-tuple-element.9), channel_id=1, source_target_pairs={{0,1},{1,2},{2,3},{3,4},{4,5},{5,6},{6,7},{7,8},{8,9},{9,10},{10,1... | collective-permute-start | bytes 23048 | tf_op jit(solution)/shard_map/ppermute | solution.py:21
  83.6 1.1 %collective-permute-done.4 = bf16[8,32,15]{2,1,0:T(8,128)(2,1)S(1)} collective-permute-done((bf16[8,32,15]{2,1,0:T(8,128)(2,1)S(1)}, bf16[8,32,15]{2,1,0:T(8,128)(2,1)S(1)}, u32[]{:S(2)}, u32[]{:S(2)}) %collective-permute-start.4) | collective-permute-done | bytes 7712 | tf_op jit(solution)/shard_map/ppermute | solution.py:21
  85.9 0.9 fusion.9
  86.9 1.9 %collective-permute-start.7 = (bf16[4,8,32,15]{3,1,2,0:T(8,128)(2,1)S(1)}, bf16[4,8,32,15]{3,1,2,0:T(8,128)(2,1)S(1)}, u32[]{:S(2)}, u32[]{:S(2)}) collective-permute-start(bf16[4,8,32,15]{3,1,2,0:T(8,128)(2,1)S(1)} %get-tuple-element.6), channel_id=1, source_target_pairs={{1,0},{2,1},{3,2},{4,3},{5,4},{6,5},{7,6},{8,7},{9,8},{10,9},{11,1... | collective-permute-start | bytes 92168 | tf_op jit(solution)/shard_map/ppermute | solution.py:23
  88.8 4.3 %collective-permute-start.6 = (bf16[4,8,32,15]{3,1,2,0:T(8,128)(2,1)S(1)}, bf16[4,8,32,15]{3,1,2,0:T(8,128)(2,1)S(1)}, u32[]{:S(2)}, u32[]{:S(2)}) collective-permute-start(bf16[4,8,32,15]{3,1,2,0:T(8,128)(2,1)S(1)} %get-tuple-element.5), channel_id=1, source_target_pairs={{0,1},{1,2},{2,3},{3,4},{4,5},{5,6},{6,7},{7,8},{8,9},{9,10},{10,1... | collective-permute-start | bytes 92168 | tf_op jit(solution)/shard_map/ppermute | solution.py:21
  93.1 2.1 %collective-permute-done.7 = bf16[4,8,32,15]{3,1,2,0:T(8,128)(2,1)S(1)} collective-permute-done((bf16[4,8,32,15]{3,1,2,0:T(8,128)(2,1)S(1)}, bf16[4,8,32,15]{3,1,2,0:T(8,128)(2,1)S(1)}, u32[]{:S(2)}, u32[]{:S(2)}) %collective-permute-start.7) | collective-permute-done | bytes 30752 | tf_op jit(solution)/shard_map/ppermute | solution.py:23
  95.2 1.9 %collective-permute-done.6 = bf16[4,8,32,15]{3,1,2,0:T(8,128)(2,1)S(1)} collective-permute-done((bf16[4,8,32,15]{3,1,2,0:T(8,128)(2,1)S(1)}, bf16[4,8,32,15]{3,1,2,0:T(8,128)(2,1)S(1)}, u32[]{:S(2)}, u32[]{:S(2)}) %collective-permute-start.6) | collective-permute-done | bytes 30752 | tf_op jit(solution)/shard_map/ppermute | solution.py:21
  (51 shorter events, 11.2 us)
Async XLA Ops:
  6.3 13.8 %copy-start = (f32[8,32,128]{2,1,0:T(8,128)S(1)}, f32[8,32,128]{2,1,0:T(8,128)}, u32[]{:S(2)}) copy-start(f32[8,32,128]{2,1,0:T(8,128)} %param.6) | copy-start | bytes 393220
  6.3 19.6 %copy-start.1 = (f32[1,4,3,31]{3,1,2,0:T(4,128)S(1)}, f32[1,4,3,31]{3,1,2,0:T(4,128)}, u32[]{:S(2)}) copy-start(f32[1,4,3,31]{3,1,2,0:T(4,128)} %param.7) | copy-start | bytes 4468
  6.3 40.3 %copy-start.3 = (s32[16]{0:T(128)S(1)}, s32[16]{0:T(128)}, u32[]{:S(2)}) copy-start(s32[16]{0:T(128)} %param.8) | copy-start | bytes 196
  6.3 43.1 %copy-start.2 = (s32[16,4]{0,1:T(4,128)S(1)}, s32[16,4]{0,1:T(4,128)}, u32[]{:S(2)}) copy-start(s32[16,4]{0,1:T(4,128)} %param.9) | copy-start | bytes 772
  12.8 39.9 %all-to-all-start = ((bf16[16,2,4096]{2,1,0:T(2,128)(2,1)}), bf16[16,2,4096]{2,1,0:T(2,128)(2,1)S(1)}, u32[]{:S(2)}, u32[]{:S(2)}) async-start(bf16[16,2,4096]{2,1,0:T(2,128)(2,1)} %reshape.127), calls=%async_computation | async-start | bytes 524288 | tf_op jit(solution)/shard_map/all_to_all | solution.py:73
  20.3 31.2 %collective-permute-start.1 = (bf16[8,32,15]{2,1,0:T(8,128)(2,1)S(1)}, bf16[8,32,15]{2,1,0:T(8,128)(2,1)S(1)}, u32[]{:S(2)}, u32[]{:S(2)}) collective-permute-start(bf16[8,32,15]{2,1,0:T(8,128)(2,1)S(1)} %get-tuple-element.12), channel_id=1, source_target_pairs={{1,0},{2,1},{3,2},{4,3},{5,4},{6,5},{7,6},{8,7},{9,8},{10,9},{11,1... | collective-permute-start | bytes 23048 | tf_op jit(solution)/shard_map/ppermute | solution.py:23
  22.3 29.2 %collective-permute-start = (bf16[8,32,15]{2,1,0:T(8,128)(2,1)S(1)}, bf16[8,32,15]{2,1,0:T(8,128)(2,1)S(1)}, u32[]{:S(2)}, u32[]{:S(2)}) collective-permute-start(bf16[8,32,15]{2,1,0:T(8,128)(2,1)S(1)} %get-tuple-element.11), channel_id=1, source_target_pairs={{0,1},{1,2},{2,3},{3,4},{4,5},{5,6},{6,7},{7,8},{8,9},{9,10},{10,1... | collective-permute-start | bytes 23048 | tf_op jit(solution)/shard_map/ppermute | solution.py:21
  65.6 7.7 %collective-permute-start.3 = (bf16[4,8,32,15]{3,1,2,0:T(8,128)(2,1)S(1)}, bf16[4,8,32,15]{3,1,2,0:T(8,128)(2,1)S(1)}, u32[]{:S(2)}, u32[]{:S(2)}) collective-permute-start(bf16[4,8,32,15]{3,1,2,0:T(8,128)(2,1)S(1)} %get-tuple-element.8), channel_id=1, source_target_pairs={{1,0},{2,1},{3,2},{4,3},{5,4},{6,5},{7,6},{8,7},{9,8},{10,9},{11,1... | collective-permute-start | bytes 92168 | tf_op jit(solution)/shard_map/ppermute | solution.py:23
  67.7 6.8 %collective-permute-start.2 = (bf16[4,8,32,15]{3,1,2,0:T(8,128)(2,1)S(1)}, bf16[4,8,32,15]{3,1,2,0:T(8,128)(2,1)S(1)}, u32[]{:S(2)}, u32[]{:S(2)}) collective-permute-start(bf16[4,8,32,15]{3,1,2,0:T(8,128)(2,1)S(1)} %get-tuple-element.7), channel_id=1, source_target_pairs={{0,1},{1,2},{2,3},{3,4},{4,5},{5,6},{6,7},{7,8},{8,9},{9,10},{10,1... | collective-permute-start | bytes 92168 | tf_op jit(solution)/shard_map/ppermute | solution.py:21
  77.1 6.5 %collective-permute-start.5 = (bf16[8,32,15]{2,1,0:T(8,128)(2,1)S(1)}, bf16[8,32,15]{2,1,0:T(8,128)(2,1)S(1)}, u32[]{:S(2)}, u32[]{:S(2)}) collective-permute-start(bf16[8,32,15]{2,1,0:T(8,128)(2,1)S(1)} %get-tuple-element.10), channel_id=1, source_target_pairs={{1,0},{2,1},{3,2},{4,3},{5,4},{6,5},{7,6},{8,7},{9,8},{10,9},{11,1... | collective-permute-start | bytes 23048 | tf_op jit(solution)/shard_map/ppermute | solution.py:23
  79.0 5.7 %collective-permute-start.4 = (bf16[8,32,15]{2,1,0:T(8,128)(2,1)S(1)}, bf16[8,32,15]{2,1,0:T(8,128)(2,1)S(1)}, u32[]{:S(2)}, u32[]{:S(2)}) collective-permute-start(bf16[8,32,15]{2,1,0:T(8,128)(2,1)S(1)} %get-tuple-element.9), channel_id=1, source_target_pairs={{0,1},{1,2},{2,3},{3,4},{4,5},{5,6},{6,7},{7,8},{8,9},{9,10},{10,1... | collective-permute-start | bytes 23048 | tf_op jit(solution)/shard_map/ppermute | solution.py:21
  86.9 8.3 %collective-permute-start.7 = (bf16[4,8,32,15]{3,1,2,0:T(8,128)(2,1)S(1)}, bf16[4,8,32,15]{3,1,2,0:T(8,128)(2,1)S(1)}, u32[]{:S(2)}, u32[]{:S(2)}) collective-permute-start(bf16[4,8,32,15]{3,1,2,0:T(8,128)(2,1)S(1)} %get-tuple-element.6), channel_id=1, source_target_pairs={{1,0},{2,1},{3,2},{4,3},{5,4},{6,5},{7,6},{8,7},{9,8},{10,9},{11,1... | collective-permute-start | bytes 92168 | tf_op jit(solution)/shard_map/ppermute | solution.py:23
  88.8 8.3 %collective-permute-start.6 = (bf16[4,8,32,15]{3,1,2,0:T(8,128)(2,1)S(1)}, bf16[4,8,32,15]{3,1,2,0:T(8,128)(2,1)S(1)}, u32[]{:S(2)}, u32[]{:S(2)}) collective-permute-start(bf16[4,8,32,15]{3,1,2,0:T(8,128)(2,1)S(1)} %get-tuple-element.5), channel_id=1, source_target_pairs={{0,1},{1,2},{2,3},{3,4},{4,5},{5,6},{6,7},{7,8},{8,9},{9,10},{10,1... | collective-permute-start | bytes 92168 | tf_op jit(solution)/shard_map/ppermute | solution.py:21
where the time goes:
time: 101 us; the launch traced here: 100 us
  starting transfers between devices  31.2 us (31%)
  local copies, waits for them, and re-layouts  25.6 us (25%)
  blocking collectives  20.7 us (20%)
  matrix products  12.2 us (12%)
  waiting for transfers between devices  7.98 us (8%)
  other arithmetic  2.37 us (2%)
    all_gather x1, blocking collectives, shards(): fitted = lax.all_gather(psf_bank, ('plane', 'brick'), axis=0, tiled=True)  20.7 us
    unnamed x11, local copies, waits for them, and re-layouts  18.8 us
    ppermute x4, starting transfers between devices, padded_2(): lax.ppermute(tail, axis, [(i, (i + 1) % count) for i in range(ends)])  15.9 us
    ppermute x4, starting transfers between devices, padded_2(): lax.ppermute(head, axis, [((i + 1) % count, i) for i in range(ends)])  7.93 us
    all_to_all x1, starting transfers between devices, shards(): lax.all_to_all(camera_rows, ('plane', 'brick'), split_axis=3, concat_axis...  7.35 us
    convert_element_type x1, local copies, waits for them, and re-layouts, shards(): regrouped.astype(jnp.float32) / (blurred + BACKGROUND)  5.93 us
    ppermute x4, waiting for transfers between devices, padded_2(): lax.ppermute(tail, axis, [(i, (i + 1) % count) for i in range(ends)])  4.22 us
    ppermute x4, waiting for transfers between devices, padded_2(): lax.ppermute(head, axis, [((i + 1) % count, i) for i in range(ends)])  3.76 us
  transfers between devices with their start and end apart: 9, of which 5 were waited for; matrix products, arithmetic and copies ran while one was open for 7% of the time, Pallas kernels for 0%

commit v1 on v0

--- a/solution.py
+++ b/solution.py
@@ -70,8 +70,14 @@
 
 
 def shards(camera_rows, estimate, psf_bank, psf_owner, view_mask):
-    regrouped = lax.all_to_all(
-        camera_rows, ("plane", "brick"), split_axis=3, concat_axis=2, tiled=True
+    regrouped = jnp.concatenate(
+        lax.all_to_all(
+            jnp.stack(jnp.split(camera_rows, lax.axis_size(("plane", "brick")), axis=3)),
+            ("plane", "brick"),
+            0,
+            0,
+        ),
+        axis=2,
     )
     position = lax.axis_index(("plane", "brick"))
     brick_ids = jnp.arange(psf_owner.shape[0], dtype=jnp.int32)

time: 101 us -> 90.2 us (0.89)
  local copies, waits for them, and re-layouts: 25.6 us -> 12.3 us
  waiting for transfers between devices: 7.98 us -> 13.2 us
  starting transfers between devices: 31.2 us -> 26.1 us
  blocking collectives: 20.7 us -> 21.9 us
  other arithmetic: 2.37 us -> 3.53 us
    ppermute x4, waiting for transfers between devices: 3.76 us -> 12.1 us  [padded_2(): lax.ppermute(head, axis, [((i + 1) % count, i) for i in range(ends)])]
    unnamed x11 -> x25, local copies, waits for them, and re-layouts: 18.8 us -> 10.7 us
    convert_element_type x1, local copies, waits for them, and re-layouts: 5.93 us -> 0.04 us  [shards(): regrouped.astype(jnp.float32) / (blurred + BACKGROUND)]
    ppermute x4, starting transfers between devices: 15.9 us -> 10.3 us  [padded_2(): lax.ppermute(tail, axis, [(i, (i + 1) % count) for i in range(ends)])]
    ppermute x4, waiting for transfers between devices: 4.22 us -> 1.09 us  [padded_2(): lax.ppermute(tail, axis, [(i, (i + 1) % count) for i in range(ends)])]
    ppermute x4, starting transfers between devices: 7.93 us -> 9.34 us  [padded_2(): lax.ppermute(head, axis, [((i + 1) % count, i) for i in range(ends)])]
    all_gather x1, blocking collectives: 20.7 us -> 21.9 us  [shards(): fitted = lax.all_gather(psf_bank, ('plane', 'brick'), axis=0, tiled=True)]
  transfers between devices with their start and end apart: 9 -> 9, of which waited for: 5 -> 5; matrix products, arithmetic and copies ran while one was open for 7% -> 20% of each run, Pallas kernels for 0% -> 0%
where the time goes in v1:
time: 90.2 us; the launch traced here: 89.5 us
  starting transfers between devices  26.1 us (29%)
  blocking collectives  21.9 us (24%)
  waiting for transfers between devices  13.2 us (15%)
  local copies, waits for them, and re-layouts  12.3 us (14%)
  matrix products  12.2 us (14%)
  other arithmetic  3.53 us (4%)
    all_gather x1, blocking collectives, shards(): fitted = lax.all_gather(psf_bank, ('plane', 'brick'), axis=0, tiled=True)  21.9 us
    ppermute x4, waiting for transfers between devices, padded_2(): lax.ppermute(head, axis, [((i + 1) % count, i) for i in range(ends)])  12.1 us
    unnamed x25, local copies, waits for them, and re-layouts  10.7 us
    ppermute x4, starting transfers between devices, padded_2(): lax.ppermute(tail, axis, [(i, (i + 1) % count) for i in range(ends)])  10.3 us
    ppermute x4, starting transfers between devices, padded_2(): lax.ppermute(head, axis, [((i + 1) % count, i) for i in range(ends)])  9.34 us
    all_to_all x1, starting transfers between devices, shards(): lax.all_to_all(jnp.stack(jnp.split(camera_rows, lax.axis_size(('plane', '...  6.45 us
    dot_general x4, matrix products, across_depth(): return jnp.einsum('vzyc,vzw->vwyc', volume, band_z, precision=HIGHEST)  3.35 us
    dot_general x6, matrix products, banded(): return jnp.einsum('ijt,vt->vij', one_hot, profiles, precision=HIGHEST)  3.14 us
  transfers between devices with their start and end apart: 9, of which 5 were waited for; matrix products, arithmetic and copies ran while one was open for 20% of the time, Pallas kernels for 0%

profile of v1, /device:TPU:1, one launch (start us, length us, event | category | flops | bytes accessed | tf_op | source)
XLA Modules:
  0.0 89.5 jit_solution(286209921248299283)
XLA Ops:
  0.0 1.0 %convert_element_type.36 = bf16[8,32,128]{2,1,0:T(8,128)(2,1)S(1)} convert(f32[8,32,128]{2,1,0:T(8,128)} %param.6) | non-fusion elementwise | flops 32768 | bytes 196608 | tf_op jit(solution)/shard_map/convert_element_type | solution.py:108
  1.1 4.5 %collective-permute-start = (bf16[8,32,15]{2,1,0:T(8,128)(2,1)S(1)}, bf16[8,32,15]{2,1,0:T(8,128)(2,1)S(1)}, u32[]{:S(2)}, u32[]{:S(2)}) collective-permute-start(bf16[8,32,15]{2,1,0:T(8,128)(2,1)S(1)} %get-tuple-element.11), channel_id=1, source_target_pairs={{0,1},{1,2},{2,3},{3,4},{4,5},{5,6},{6,7},{7,8},{8,9},{9,10},{10,1... | collective-permute-start | bytes 23048 | tf_op jit(solution)/shard_map/ppermute | solution.py:21
  5.6 1.9 %collective-permute-start.1 = (bf16[8,32,15]{2,1,0:T(8,128)(2,1)S(1)}, bf16[8,32,15]{2,1,0:T(8,128)(2,1)S(1)}, u32[]{:S(2)}, u32[]{:S(2)}) collective-permute-start(bf16[8,32,15]{2,1,0:T(8,128)(2,1)S(1)} %get-tuple-element.12), channel_id=1, source_target_pairs={{1,0},{2,1},{3,2},{4,3},{5,4},{6,5},{7,6},{8,7},{9,8},{10,9},{11,1... | collective-permute-start | bytes 23048 | tf_op jit(solution)/shard_map/ppermute | solution.py:23
  7.5 1.3 %constant_dynamic-update-slice_fusion.15 = bf16[16,4,8,2,128]{4,3,2,1,0:T(2,128)(2,1)} fusion(bf16[4,8,2,2048]{3,2,1,0:T(2,128)(2,1)} %param.5), kind=kLoop, calls=%fused_computation.100 | loop fusion | bytes 32768
  8.9 1.3 %constant_dynamic-update-slice_fusion.14 = bf16[16,4,8,2,128]{4,3,2,1,0:T(2,128)(2,1)} fusion(bf16[16,4,8,2,128]{4,3,2,1,0:T(2,128)(2,1)} %constant_dynamic-update-slice_fusion.15, bf16[4,8,2,2048]{3,2,1,0:T(2,128)(2,1)} %param.5), kind=kLoop, calls=%fused_computation.99 | loop fusion | bytes 32768
  18.8 6.5 %all-to-all-start = ((bf16[16,4,8,2,128]{4,3,2,1,0:T(2,128)(2,1)}), bf16[16,4,8,2,128]{4,3,2,1,0:T(2,128)(2,1)S(1)}, u32[]{:S(2)}, u32[]{:S(2)}) async-start(bf16[16,4,8,2,128]{4,3,2,1,0:T(2,128)(2,1)} %constant_dynamic-update-slice_fusion), calls=%async_computation | async-start | bytes 524288 | tf_op jit(solution)/shard_map/all_to_all | solution.py:74
  25.9 21.9 %all_gather.3 = f32[16,4,3,31]{3,1,2,0:T(4,128)S(1)} all-gather(f32[1,4,3,31]{3,1,2,0:T(4,128)S(1)} %copy-done.2), channel_id=1, replica_groups=mesh['slab'=2,'plane'=8,'brick'=2] {'plane','brick'}, dimensions={0}, use_global_device_ids=true | all-gather | bytes 25296 | tf_op jit(solution)/shard_map/all_gather | solution.py:87
  47.8 0.8 fusion.48
  48.8 0.9 %fusion.12 = f32[4,158,128,1]{2,0,1,3:T(4,128)S(1)} fusion(s32[158,128]{1,0:T(8,128)S(1)} %iota_subtract_fusion, f32[4,3,31]{2,0,1:T(4,128)S(1)} %bitcast_divide_fusion), kind=kOutput, calls=%fused_computation.33 | convolution fusion | flops 30720256 | bytes 407552 | tf_op jit(solution)/shard_map/ijt,vt->vij/dot_general | solution.py:42
  50.2 0.9 %fusion.13 = f32[4,158,128,1]{2,0,1,3:T(4,128)S(1)} fusion(s32[158,128]{1,0:T(8,128)S(1)} %iota_subtract_fusion, f32[4,1,31]{2,0,1:T(4,128)S(1)} %slice.54), kind=kOutput, calls=%fused_computation.34 | convolution fusion | flops 30720256 | bytes 404976 | tf_op jit(solution)/shard_map/ijt,vt->vij/dot_general | solution.py:42
  53.6 0.9 fusion.8
  54.6 1.9 %collective-permute-start.2 = (bf16[4,8,32,15]{3,1,2,0:T(8,128)(2,1)S(1)}, bf16[4,8,32,15]{3,1,2,0:T(8,128)(2,1)S(1)}, u32[]{:S(2)}, u32[]{:S(2)}) collective-permute-start(bf16[4,8,32,15]{3,1,2,0:T(8,128)(2,1)S(1)} %get-tuple-element.7), channel_id=1, source_target_pairs={{0,1},{1,2},{2,3},{3,4},{4,5},{5,6},{6,7},{7,8},{8,9},{9,10},{10,1... | collective-permute-start | bytes 92168 | tf_op jit(solution)/shard_map/ppermute | solution.py:21
  56.5 2.4 %collective-permute-start.3 = (bf16[4,8,32,15]{3,1,2,0:T(8,128)(2,1)S(1)}, bf16[4,8,32,15]{3,1,2,0:T(8,128)(2,1)S(1)}, u32[]{:S(2)}, u32[]{:S(2)}) collective-permute-start(bf16[4,8,32,15]{3,1,2,0:T(8,128)(2,1)S(1)} %get-tuple-element.8), channel_id=1, source_target_pairs={{1,0},{2,1},{3,2},{4,3},{5,4},{6,5},{7,6},{8,7},{9,8},{10,9},{11,1... | collective-permute-start | bytes 92168 | tf_op jit(solution)/shard_map/ppermute | solution.py:23
  59.8 4.4 %collective-permute-done.3 = bf16[4,8,32,15]{3,1,2,0:T(8,128)(2,1)S(1)} collective-permute-done((bf16[4,8,32,15]{3,1,2,0:T(8,128)(2,1)S(1)}, bf16[4,8,32,15]{3,1,2,0:T(8,128)(2,1)S(1)}, u32[]{:S(2)}, u32[]{:S(2)}) %collective-permute-start.3) | collective-permute-done | bytes 30752 | tf_op jit(solution)/shard_map/ppermute | solution.py:23
  65.8 0.8 fusion.10
  66.9 1.9 %collective-permute-start.4 = (bf16[8,32,15]{2,1,0:T(8,128)(2,1)S(1)}, bf16[8,32,15]{2,1,0:T(8,128)(2,1)S(1)}, u32[]{:S(2)}, u32[]{:S(2)}) collective-permute-start(bf16[8,32,15]{2,1,0:T(8,128)(2,1)S(1)} %get-tuple-element.9), channel_id=1, source_target_pairs={{0,1},{1,2},{2,3},{3,4},{4,5},{5,6},{6,7},{7,8},{8,9},{9,10},{10,1... | collective-permute-start | bytes 23048 | tf_op jit(solution)/shard_map/ppermute | solution.py:21
  68.8 2.4 %collective-permute-start.5 = (bf16[8,32,15]{2,1,0:T(8,128)(2,1)S(1)}, bf16[8,32,15]{2,1,0:T(8,128)(2,1)S(1)}, u32[]{:S(2)}, u32[]{:S(2)}) collective-permute-start(bf16[8,32,15]{2,1,0:T(8,128)(2,1)S(1)} %get-tuple-element.10), channel_id=1, source_target_pairs={{1,0},{2,1},{3,2},{4,3},{5,4},{6,5},{7,6},{8,7},{9,8},{10,9},{11,1... | collective-permute-start | bytes 23048 | tf_op jit(solution)/shard_map/ppermute | solution.py:23
  71.2 3.2 %collective-permute-done.5 = bf16[8,32,15]{2,1,0:T(8,128)(2,1)S(1)} collective-permute-done((bf16[8,32,15]{2,1,0:T(8,128)(2,1)S(1)}, bf16[8,32,15]{2,1,0:T(8,128)(2,1)S(1)}, u32[]{:S(2)}, u32[]{:S(2)}) %collective-permute-start.5) | collective-permute-done | bytes 7712 | tf_op jit(solution)/shard_map/ppermute | solution.py:23
  75.6 0.9 fusion.9
  76.6 1.9 %collective-permute-start.6 = (bf16[4,8,32,15]{3,1,2,0:T(8,128)(2,1)S(1)}, bf16[4,8,32,15]{3,1,2,0:T(8,128)(2,1)S(1)}, u32[]{:S(2)}, u32[]{:S(2)}) collective-permute-start(bf16[4,8,32,15]{3,1,2,0:T(8,128)(2,1)S(1)} %get-tuple-element.5), channel_id=1, source_target_pairs={{0,1},{1,2},{2,3},{3,4},{4,5},{5,6},{6,7},{7,8},{8,9},{9,10},{10,1... | collective-permute-start | bytes 92168 | tf_op jit(solution)/shard_map/ppermute | solution.py:21
  78.5 2.6 %collective-permute-start.7 = (bf16[4,8,32,15]{3,1,2,0:T(8,128)(2,1)S(1)}, bf16[4,8,32,15]{3,1,2,0:T(8,128)(2,1)S(1)}, u32[]{:S(2)}, u32[]{:S(2)}) collective-permute-start(bf16[4,8,32,15]{3,1,2,0:T(8,128)(2,1)S(1)} %get-tuple-element.6), channel_id=1, source_target_pairs={{1,0},{2,1},{3,2},{4,3},{5,4},{6,5},{7,6},{8,7},{9,8},{10,9},{11,1... | collective-permute-start | bytes 92168 | tf_op jit(solution)/shard_map/ppermute | solution.py:23
  81.8 4.6 %collective-permute-done.7 = bf16[4,8,32,15]{3,1,2,0:T(8,128)(2,1)S(1)} collective-permute-done((bf16[4,8,32,15]{3,1,2,0:T(8,128)(2,1)S(1)}, bf16[4,8,32,15]{3,1,2,0:T(8,128)(2,1)S(1)}, u32[]{:S(2)}, u32[]{:S(2)}) %collective-permute-start.7) | collective-permute-done | bytes 30752 | tf_op jit(solution)/shard_map/ppermute | solution.py:23
  88.0 0.8 fusion.11
  88.8 0.7 fusion.46
  (67 shorter events, 18.8 us)
Async XLA Ops:
  0.0 10.2 %copy-start.1 = (bf16[4,8,2,2048]{3,2,1,0:T(2,128)(2,1)S(1)}, bf16[4,8,2,2048]{3,2,1,0:T(2,128)(2,1)}, u32[]{:S(2)}) copy-start(bf16[4,8,2,2048]{3,2,1,0:T(2,128)(2,1)} %param.5) | copy-start | bytes 786436
  1.1 51.0 %collective-permute-start = (bf16[8,32,15]{2,1,0:T(8,128)(2,1)S(1)}, bf16[8,32,15]{2,1,0:T(8,128)(2,1)S(1)}, u32[]{:S(2)}, u32[]{:S(2)}) collective-permute-start(bf16[8,32,15]{2,1,0:T(8,128)(2,1)S(1)} %get-tuple-element.11), channel_id=1, source_target_pairs={{0,1},{1,2},{2,3},{3,4},{4,5},{5,6},{6,7},{7,8},{8,9},{9,10},{10,1... | collective-permute-start | bytes 23048 | tf_op jit(solution)/shard_map/ppermute | solution.py:21
  5.6 46.5 %collective-permute-start.1 = (bf16[8,32,15]{2,1,0:T(8,128)(2,1)S(1)}, bf16[8,32,15]{2,1,0:T(8,128)(2,1)S(1)}, u32[]{:S(2)}, u32[]{:S(2)}) collective-permute-start(bf16[8,32,15]{2,1,0:T(8,128)(2,1)S(1)} %get-tuple-element.12), channel_id=1, source_target_pairs={{1,0},{2,1},{3,2},{4,3},{5,4},{6,5},{7,6},{8,7},{9,8},{10,9},{11,1... | collective-permute-start | bytes 23048 | tf_op jit(solution)/shard_map/ppermute | solution.py:23
  11.4 13.9 %copy-start.4 = (s32[16]{0:T(128)S(1)}, s32[16]{0:T(128)}, u32[]{:S(2)}) copy-start(s32[16]{0:T(128)} %param.8) | copy-start | bytes 196
  11.4 14.5 %copy-start.2 = (f32[1,4,3,31]{3,1,2,0:T(4,128)S(1)}, f32[1,4,3,31]{3,1,2,0:T(4,128)}, u32[]{:S(2)}) copy-start(f32[1,4,3,31]{3,1,2,0:T(4,128)} %param.7) | copy-start | bytes 4468
  18.8 34.5 %all-to-all-start = ((bf16[16,4,8,2,128]{4,3,2,1,0:T(2,128)(2,1)}), bf16[16,4,8,2,128]{4,3,2,1,0:T(2,128)(2,1)S(1)}, u32[]{:S(2)}, u32[]{:S(2)}) async-start(bf16[16,4,8,2,128]{4,3,2,1,0:T(2,128)(2,1)} %constant_dynamic-update-slice_fusion), calls=%async_computation | async-start | bytes 524288 | tf_op jit(solution)/shard_map/all_to_all | solution.py:74
  25.2 24.7 %copy-start.3 = (s32[16,4]{0,1:T(4,128)S(1)}, s32[16,4]{0,1:T(4,128)}, u32[]{:S(2)}) copy-start(s32[16,4]{0,1:T(4,128)} %param.9) | copy-start | bytes 772
  54.6 5.2 %collective-permute-start.2 = (bf16[4,8,32,15]{3,1,2,0:T(8,128)(2,1)S(1)}, bf16[4,8,32,15]{3,1,2,0:T(8,128)(2,1)S(1)}, u32[]{:S(2)}, u32[]{:S(2)}) collective-permute-start(bf16[4,8,32,15]{3,1,2,0:T(8,128)(2,1)S(1)} %get-tuple-element.7), channel_id=1, source_target_pairs={{0,1},{1,2},{2,3},{3,4},{4,5},{5,6},{6,7},{7,8},{8,9},{9,10},{10,1... | collective-permute-start | bytes 92168 | tf_op jit(solution)/shard_map/ppermute | solution.py:21
  56.5 7.7 %collective-permute-start.3 = (bf16[4,8,32,15]{3,1,2,0:T(8,128)(2,1)S(1)}, bf16[4,8,32,15]{3,1,2,0:T(8,128)(2,1)S(1)}, u32[]{:S(2)}, u32[]{:S(2)}) collective-permute-start(bf16[4,8,32,15]{3,1,2,0:T(8,128)(2,1)S(1)} %get-tuple-element.8), channel_id=1, source_target_pairs={{1,0},{2,1},{3,2},{4,3},{5,4},{6,5},{7,6},{8,7},{9,8},{10,9},{11,1... | collective-permute-start | bytes 92168 | tf_op jit(solution)/shard_map/ppermute | solution.py:23
  65.8 0.9 %copy-start = (f32[8,32,128]{2,1,0:T(8,128)S(1)}, f32[8,32,128]{2,1,0:T(8,128)}, u32[]{:S(2)}) copy-start(f32[8,32,128]{2,1,0:T(8,128)} %param.6) | copy-start | bytes 393220
  66.9 4.3 %collective-permute-start.4 = (bf16[8,32,15]{2,1,0:T(8,128)(2,1)S(1)}, bf16[8,32,15]{2,1,0:T(8,128)(2,1)S(1)}, u32[]{:S(2)}, u32[]{:S(2)}) collective-permute-start(bf16[8,32,15]{2,1,0:T(8,128)(2,1)S(1)} %get-tuple-element.9), channel_id=1, source_target_pairs={{0,1},{1,2},{2,3},{3,4},{4,5},{5,6},{6,7},{7,8},{8,9},{9,10},{10,1... | collective-permute-start | bytes 23048 | tf_op jit(solution)/shard_map/ppermute | solution.py:21
  68.8 5.6 %collective-permute-start.5 = (bf16[8,32,15]{2,1,0:T(8,128)(2,1)S(1)}, bf16[8,32,15]{2,1,0:T(8,128)(2,1)S(1)}, u32[]{:S(2)}, u32[]{:S(2)}) collective-permute-start(bf16[8,32,15]{2,1,0:T(8,128)(2,1)S(1)} %get-tuple-element.10), channel_id=1, source_target_pairs={{1,0},{2,1},{3,2},{4,3},{5,4},{6,5},{7,6},{8,7},{9,8},{10,9},{11,1... | collective-permute-start | bytes 23048 | tf_op jit(solution)/shard_map/ppermute | solution.py:23
  76.6 5.2 %collective-permute-start.6 = (bf16[4,8,32,15]{3,1,2,0:T(8,128)(2,1)S(1)}, bf16[4,8,32,15]{3,1,2,0:T(8,128)(2,1)S(1)}, u32[]{:S(2)}, u32[]{:S(2)}) collective-permute-start(bf16[4,8,32,15]{3,1,2,0:T(8,128)(2,1)S(1)} %get-tuple-element.5), channel_id=1, source_target_pairs={{0,1},{1,2},{2,3},{3,4},{4,5},{5,6},{6,7},{7,8},{8,9},{9,10},{10,1... | collective-permute-start | bytes 92168 | tf_op jit(solution)/shard_map/ppermute | solution.py:21
  78.5 7.8 %collective-permute-start.7 = (bf16[4,8,32,15]{3,1,2,0:T(8,128)(2,1)S(1)}, bf16[4,8,32,15]{3,1,2,0:T(8,128)(2,1)S(1)}, u32[]{:S(2)}, u32[]{:S(2)}) collective-permute-start(bf16[4,8,32,15]{3,1,2,0:T(8,128)(2,1)S(1)} %get-tuple-element.6), channel_id=1, source_target_pairs={{1,0},{2,1},{3,2},{4,3},{5,4},{6,5},{7,6},{8,7},{9,8},{10,9},{11,1... | collective-permute-start | bytes 92168 | tf_op jit(solution)/shard_map/ppermute | solution.py:23
